TPU v7x, 32 devices: a whole 2x2x4 slice. The times are simulated.
32 devices in a mesh: img: 2 (over y), tile: 16 (over z, x, core).
Axes of the slice: x: 2, y: 2, z: 4, core: 2. Of those that a mesh axis runs over, the one named last changes fastest.
Arguments:
- means: float32 [3, 65536], P(None, ('img', 'tile')), may hold values from -3 to 3
- log_scales: float32 [3, 65536], P(None, ('img', 'tile')), may hold values from -6 to -3
- quat_w: float32 [1, 65536], P(None, ('img', 'tile')), may hold values from 1 to 2
- quat_v: float32 [3, 65536], P(None, ('img', 'tile')), may hold values from -1 to 1
- opacity: float32 [1, 65536], P(None, ('img', 'tile')), may hold values from -6 to 6
- sh_coeffs: float32 [48, 65536], P(None, ('img', 'tile')), may hold values from -3 to 3
- cameras: float32 [2, 10], replicated, may hold values from -300 to 300
- requests: int32 [2, 16, 2, 16, 16], P('img', 'tile'), may hold values from 0 to 2047, as said below
- lists: int32 [2, 128, 256], P('img', 'tile'), may hold values from 0 to 511, as said below
- counts: int32 [2, 128], P('img', 'tile'), may hold values from 1 to 256
- image_cot: float32 [2, 3, 128, 256], P('img', None, 'tile'), may hold values from -6 to 6
Outputs:
- rendered: float32 [2, 3, 128, 256], P('img', None, 'tile')
- param_grad: float32 [59, 65536], P(None, ('img', 'tile'))
- camera_grad: float32 [2, 10], replicated
Inputs may be any that keep to these rules, and one draw needn't show every extreme that they name: Entries may repeat within a device's requests. `lists`: each entry names a request slot of the device that renders the tile; slot (a * 16 + b) * 16 + c is requests[i, t, a, b, c]; only the first counts entries of a list are live.
All inputs are finite; a program needn't handle non-finite values.
Results may differ from a plain program's by a relative error of at most 0.0003.
Values sent between devices are 32-bit elements; how exact they have to be, the bound alone decides.
A program may use at most 64 MiB of HBM per device.

v0:
```python
import functools
import math

import jax
import jax.numpy as jnp
from jax import lax
from jax.experimental import pallas as pl
from jax.experimental.pallas import tpu as pltpu
from jax.sharding import PartitionSpec as P

TILE_SIDE = 16
TW = 16
NFEAT = 9
NSENT = 24
NBACK = 16
LANES = 128
F32 = jnp.float32
BF16 = jnp.bfloat16
MESH = pl.DeviceIdType.MESH

sh_first = 0.28209479177387814
sh_second = 0.4886025119029199
sh_third = (
    1.0925484305920792,
    -1.0925484305920792,
    0.31539156525252005,
    -1.0925484305920792,
    0.5462742152960396,
)
sh_fourth = (
    -0.5900435899266435,
    2.890611442640554,
    -0.4570457994644658,
    0.3731763325901154,
    -0.4570457994644658,
    1.445305721320277,
    -0.5900435899266435,
)
dilation = 0.3


def harmonics(x, y, z):
    xx, yy, zz = x * x, y * y, z * z
    zero = jnp.zeros_like(x)
    a, b = sh_third, sh_fourth
    c = sh_second
    values = [
        zero + sh_first,
        -c * y,
        c * z,
        -c * x,
        a[0] * x * y,
        a[1] * y * z,
        a[2] * (2.0 * zz - xx - yy),
        a[3] * x * z,
        a[4] * (xx - yy),
        b[0] * y * (3.0 * xx - yy),
        b[1] * x * y * z,
        b[2] * y * (4.0 * zz - xx - yy),
        b[3] * z * (2.0 * zz - 3.0 * xx - 3.0 * yy),
        b[4] * x * (4.0 * zz - xx - yy),
        b[5] * z * (xx - yy),
        b[6] * x * (xx - 3.0 * yy),
    ]
    by_x = [
        zero,
        zero,
        zero,
        zero - c,
        a[0] * y,
        zero,
        -2.0 * a[2] * x,
        a[3] * z,
        2.0 * a[4] * x,
        6.0 * b[0] * x * y,
        b[1] * y * z,
        -2.0 * b[2] * x * y,
        -6.0 * b[3] * x * z,
        b[4] * (4.0 * zz - 3.0 * xx - yy),
        2.0 * b[5] * x * z,
        b[6] * (3.0 * xx - 3.0 * yy),
    ]
    by_y = [
        zero,
        zero - c,
        zero,
        zero,
        a[0] * x,
        a[1] * z,
        -2.0 * a[2] * y,
        zero,
        -2.0 * a[4] * y,
        b[0] * (3.0 * xx - 3.0 * yy),
        b[1] * x * z,
        b[2] * (4.0 * zz - xx - 3.0 * yy),
        -6.0 * b[3] * y * z,
        -2.0 * b[4] * x * y,
        -2.0 * b[5] * y * z,
        -6.0 * b[6] * x * y,
    ]
    by_z = [
        zero,
        zero,
        zero + c,
        zero,
        zero,
        a[1] * y,
        4.0 * a[2] * z,
        a[3] * x,
        zero,
        zero,
        b[1] * x * y,
        8.0 * b[2] * y * z,
        b[3] * (6.0 * zz - 3.0 * xx - 3.0 * yy),
        8.0 * b[4] * x * z,
        b[5] * (xx - yy),
        zero,
    ]
    return values, by_x, by_y, by_z


def split(value, parts):
    terms, rest = [], value
    for at in range(parts):
        term = rest.astype(BF16).astype(F32)
        terms.append(term)
        if at < parts - 1:
            rest = rest - term
    return terms


def dot(a, b):
    return jnp.dot(a, b, preferred_element_type=F32)


def dot_nt(a, b):
    return lax.dot_general(a, b, (((1,), (1,)), ((), ())), preferred_element_type=F32)


def conic(cam, sigma):
    a0, a1 = cam[0:3], cam[3:6]

    def times(a):
        return (
            a[0] * sigma[0] + a[1] * sigma[1] + a[2] * sigma[2],
            a[0] * sigma[1] + a[1] * sigma[3] + a[2] * sigma[4],
            a[0] * sigma[2] + a[1] * sigma[4] + a[2] * sigma[5],
        )

    v0, v1 = times(a0), times(a1)
    s00 = a0[0] * v0[0] + a0[1] * v0[1] + a0[2] * v0[2] + dilation
    s01 = a1[0] * v0[0] + a1[1] * v0[1] + a1[2] * v0[2]
    s11 = a1[0] * v1[0] + a1[1] * v1[1] + a1[2] * v1[2] + dilation
    inverse = 1.0 / (s00 * s11 - s01 * s01)
    return v0, v1, (s11 * inverse, -s01 * inverse, s00 * inverse)


def cov_grad(con, grad):
    ca, cb, cc = con
    ga, gb, gc = grad[0], 0.5 * grad[1], grad[2]
    p00, p01 = ca * ga + cb * gb, ca * gb + cb * gc
    p10, p11 = cb * ga + cc * gb, cb * gb + cc * gc
    return (
        -(p00 * ca + p01 * cb),
        -(p00 * cb + p01 * cc),
        -(p10 * cb + p11 * cc),
    )


def rotation_of(quat):
    w, x, y, z = quat
    return (
        (1.0 - 2.0 * (y * y + z * z), 2.0 * (x * y - w * z), 2.0 * (x * z + w * y)),
        (2.0 * (x * y + w * z), 1.0 - 2.0 * (x * x + z * z), 2.0 * (y * z - w * x)),
        (2.0 * (x * z - w * y), 2.0 * (y * z + w * x), 1.0 - 2.0 * (x * x + y * y)),
    )


def load_dense(refs, dense):
    at = 0
    for ref in refs:
        rows, owned = ref.shape
        high = owned // LANES
        for h in range(high):
            part = ref[:, h * LANES : (h + 1) * LANES]
            if rows == 1:
                dense[at * high + h : at * high + h + 1, :] = part
            else:
                dense[pl.ds(at * high + h, rows, stride=high), :] = part
        at += rows


def geometry(row):
    raw = tuple(row(6 + a) for a in range(4))
    inverse = 1.0 / jnp.sqrt(
        raw[0] * raw[0] + raw[1] * raw[1] + raw[2] * raw[2] + raw[3] * raw[3]
    )
    quat = tuple(part * inverse for part in raw)
    rot = rotation_of(quat)
    squares = tuple(jnp.exp(2.0 * row(3 + a)) for a in range(3))

    def entry(a, b):
        return (
            rot[a][0] * rot[b][0] * squares[0]
            + rot[a][1] * rot[b][1] * squares[1]
            + rot[a][2] * rot[b][2] * squares[2]
        )

    sigma = tuple(entry(a, b) for a, b in ((0, 0), (0, 1), (0, 2), (1, 1), (1, 2), (2, 2)))
    return quat, inverse, rot, squares, sigma


def mask_of(index, rows):
    return lax.broadcasted_iota(jnp.int32, (rows, index.shape[1]), 0) == index


def as_bf16(mask):
    return mask.astype(F32).astype(BF16)


def two(value):
    hi = value.astype(BF16)
    return hi, (value - hi.astype(F32)).astype(BF16)


def scatter_rows(ref, start, stride, value):
    for h in range(ref.shape[0]):
        ref[h, pl.ds(start, value.shape[0], stride=stride), :] = value[
            :, h * LANES : (h + 1) * LANES
        ]


def take_rows(ref, rows):
    return jnp.concatenate([ref[h, rows, :] for h in range(ref.shape[0])], axis=1)


def render_kernel(
    sizes,
    means,
    log_scales,
    quat_w,
    quat_v,
    opacity,
    sh,
    cams,
    requests,
    lists,
    counts,
    cot,
    rendered,
    back_out,
    ask_out,
    harm_out,
    ask_recv,
    feat_send,
    feat_recv,
    grad_send,
    grad_recv,
    dense,
    project,
    feats,
    slots,
    by_slot,
    low,
    gots,
    coefs,
    colours,
    cots,
    cots_t,
    live_op,
    moments,
    tints,
    grads,
    harm,
    send_sem,
    recv_sem,
    own_sem,
):
    n_img, n_tile, cap, tiles_here, length, pix = sizes
    owned = means.shape[1]
    high = owned // LANES
    devices = n_img * n_tile
    n_slots = devices * cap
    groups = n_slots // LANES
    per_img = n_tile * cap
    my_tile = lax.axis_index("tile")
    my_img = lax.axis_index("img")
    me = my_img * n_tile + my_tile

    def peer(k):
        other = lax.rem(me + k, devices)
        return other, (other // n_tile, lax.rem(other, n_tile))

    barrier = pltpu.get_barrier_semaphore()

    @pl.loop(1, devices)
    def _(k):
        pl.semaphore_signal(barrier, inc=1, device_id=peer(k)[1], device_id_type=MESH)

    def exchange(at, source, target):
        mine = pltpu.make_async_copy(source.at[me], target.at[me], own_sem.at[at])
        mine.start()

        @pl.loop(1, devices)
        def _(k):
            other, where = peer(k)
            pltpu.make_async_remote_copy(
                src_ref=source.at[other],
                dst_ref=target.at[me],
                send_sem=send_sem.at[at],
                recv_sem=recv_sem.at[at],
                device_id=where,
                device_id_type=MESH,
            ).start()

        return mine

    def arrive(at, target, mine):
        mine.wait()
        others = target.at[pl.ds(0, devices - 1)]
        pltpu.make_async_copy(others, others, recv_sem.at[at]).wait()

    def sent(at, source):
        others = source.at[pl.ds(0, devices - 1)]
        pltpu.make_async_copy(others, others, send_sem.at[at]).wait()

    load_dense((means, log_scales, quat_w, quat_v, opacity, sh), dense)
    cam = [[cams[i, c] for c in range(10)] for i in range(n_img)]
    row16 = lax.broadcasted_iota(jnp.int32, (16, LANES), 0)
    for i in range(n_img):
        polar = jnp.full((16, LANES), cam[i][8], F32)
        azimuth = jnp.full((16, LANES), cam[i][9], F32)
        sp, cp = jnp.sin(polar), jnp.cos(polar)
        sz, cz = jnp.sin(azimuth), jnp.cos(azimuth)
        values, by_x, by_y, by_z = harmonics(sp * cz, sp * sz, cp)
        y_col = jnp.zeros((16, LANES), F32)
        p_col = jnp.zeros((16, LANES), F32)
        z_col = jnp.zeros((16, LANES), F32)
        for m in range(16):
            here = row16 == m
            y_col = jnp.where(here, values[m], y_col)
            p_col = jnp.where(here, by_x[m] * cp * cz + by_y[m] * cp * sz - by_z[m] * sp, p_col)
            z_col = jnp.where(here, -by_x[m] * sp * sz + by_y[m] * sp * cz, z_col)
        harm[i, 0] = y_col
        harm[i, 1] = p_col
        harm[i, 2] = z_col
        harm_out[i] = y_col

    pl.semaphore_wait(barrier, devices - 1)
    asking = exchange(0, requests, ask_recv)

    def row(at):
        return dense[at * high : (at + 1) * high, :]

    _, _, _, _, sigma = geometry(row)
    mean = tuple(row(a) for a in range(3))
    base = 1.0 / (1.0 + jnp.exp(-row(10)))
    for i in range(n_img):
        c = cam[i]
        _, _, con = conic(c, sigma)
        rows = [
            c[0] * mean[0] + c[1] * mean[1] + c[2] * mean[2] + c[6],
            c[3] * mean[0] + c[4] * mean[1] + c[5] * mean[2] + c[7],
            con[0],
            con[1],
            con[2],
            base,
        ]
        sums = [[None] * 3 for _ in range(3)]
        for k in range(3):
            for m in range(16):
                coeff = row(11 + 16 * k + m)
                for d in range(3):
                    term = coeff * harm[i, d, m : m + 1, :]
                    sums[d][k] = term if m == 0 else sums[d][k] + term
        rows += [total + 0.5 for total in sums[0]] + list(mean) + list(sigma) + sums[1] + sums[2]
        for at, value in enumerate(rows):
            project[pl.ds(at, high, stride=NSENT), :] = value
        for at, term in enumerate(split(project[0 : high * NSENT, :], 3)):
            feats[i, :, at * LANES : (at + 1) * LANES] = term.astype(BF16)

    coefs[...] = jnp.zeros_like(coefs)
    colours[...] = jnp.zeros_like(colours)
    for j in range(tiles_here):
        low[j] = as_bf16(mask_of(jnp.bitwise_and(lists[j : j + 1, :], LANES - 1), LANES))
        cot3 = jnp.concatenate([cot[0, k, j : j + 1, :] for k in range(3)], axis=0)
        c1, c2, c3 = split(cot3, 3)
        stack = jnp.concatenate([c1, c1, c2, c2, c1, c3, jnp.zeros((14, pix), F32)], axis=0)
        cots[j] = stack.astype(BF16)
        cots_t[j] = jnp.transpose(stack).astype(BF16)

    def basis_of(pixel, which):
        half = 0.5 * TILE_SIDE - 0.5
        x = lax.rem(pixel, TILE_SIDE).astype(F32) - half
        y = (pixel // TILE_SIDE).astype(F32) - half
        out = jnp.where(which == 0, 1.0, 0.0)
        for at, term in enumerate((x, y, x * x, x * y, y * y)):
            out = jnp.where(which == at + 1, term, out)
        return out.astype(BF16)

    basis_pe = basis_of(
        lax.broadcasted_iota(jnp.int32, (pix, 32), 0),
        lax.rem(lax.broadcasted_iota(jnp.int32, (pix, 32), 1), 8),
    )
    basis_ep = basis_of(
        lax.broadcasted_iota(jnp.int32, (16, pix), 1), lax.broadcasted_iota(jnp.int32, (16, pix), 0)
    )
    first = lax.broadcasted_iota(jnp.int32, (length, length), 0)
    second = lax.broadcasted_iota(jnp.int32, (length, length), 1)
    before = as_bf16(first < second)
    after = as_bf16(first > second)
    height = TILE_SIDE * tiles_here * n_tile / TW

    arrive(0, ask_recv, asking)
    asks = ask_recv[...].reshape(devices, cap)
    halves = jnp.concatenate(
        [(asks // LANES).astype(F32), jnp.bitwise_and(asks, LANES - 1).astype(F32)], axis=0
    ).astype(BF16)
    repeat = as_bf16(
        lax.rem(lax.broadcasted_iota(jnp.int32, (cap, n_slots), 1), cap)
        == lax.broadcasted_iota(jnp.int32, (cap, n_slots), 0)
    )
    wide = dot(halves, repeat)
    here = (
        lax.broadcasted_iota(jnp.int32, (devices, n_slots), 1) // cap
        == lax.broadcasted_iota(jnp.int32, (devices, n_slots), 0)
    )
    ask_hi, ask_lo = (
        jnp.sum(
            jnp.where(here, wide[at * devices : (at + 1) * devices], 0.0), axis=0, keepdims=True
        ).astype(jnp.int32)
        for at in range(2)
    )
    ask_out[0:1, :] = ask_hi
    ask_out[1:2, :] = ask_lo
    for i in range(n_img):
        lanes = slice(i * per_img, (i + 1) * per_img)
        mask = as_bf16(mask_of(ask_lo[:, lanes], LANES))
        got = dot(feats[i], jnp.concatenate([mask] * 3, axis=0))
        pick = mask_of(ask_hi[:, lanes], high).astype(F32)
        total = got[0:NSENT] * pick[0:1]
        for h in range(1, high):
            total = total + got[h * NSENT : (h + 1) * NSENT] * pick[h : h + 1]
        slots[lanes, 0:NSENT] = jnp.transpose(total)
    feat_send[...] = jnp.concatenate(
        [slots[pl.ds(c, devices, stride=cap), 0:NSENT] for c in range(cap)], axis=1
    ).reshape(devices, 1, cap * NSENT)
    sending = exchange(1, feat_send, feat_recv)
    sent(0, ask_recv)
    arrive(1, feat_recv, sending)
    packed = feat_recv[...].reshape(devices, cap * NSENT)
    for c in range(cap):
        slots[pl.ds(c, devices, stride=cap), 0:NSENT] = packed[:, c * NSENT : (c + 1) * NSENT]
    heads = []
    for h in range(groups):
        turned = jnp.transpose(slots[h * LANES : (h + 1) * LANES, :])[0:NSENT]
        by_slot[h * NSENT : (h + 1) * NSENT, :] = turned
        heads.append(turned[0:16])
    heads = jnp.concatenate(
        [term.astype(BF16) for term in split(jnp.concatenate(heads, axis=0), 3)], axis=1
    )

    for j in range(tiles_here):
        got = dot(heads, jnp.concatenate([low[j]] * 3, axis=0))
        group = lists[j : j + 1, :] // LANES
        total = jnp.where(group == 0, got[0:16], 0.0)
        for h in range(1, groups):
            total = total + jnp.where(group == h, got[h * 16 : (h + 1) * 16], 0.0)
        scatter_rows(gots, j, tiles_here, total)

    def feature(at):
        return take_rows(gots, slice(at * tiles_here, (at + 1) * tiles_here))

    tile_row = lax.broadcasted_iota(jnp.int32, (tiles_here, length), 0)
    number = my_tile * tiles_here + tile_row
    lx = feature(0) - (
        (lax.rem(number, TW) * TILE_SIDE).astype(F32) + 0.5 * TILE_SIDE * (1 - TW)
    )
    ly = feature(1) - ((number // TW * TILE_SIDE).astype(F32) + 0.5 * TILE_SIDE - 0.5 * height)
    ca, cb, cc, op = (feature(at) for at in range(2, 6))
    ux = ca * lx + cb * ly
    uy = cc * ly + cb * lx
    live = jnp.zeros((tiles_here, length), jnp.int32)
    for j in range(tiles_here):
        live = jnp.where(tile_row == j, counts[0, j], live)
    lane = lax.broadcasted_iota(jnp.int32, (tiles_here, length), 1)
    live_op[...] = jnp.where(lane < live, op, 0.0)
    for at, value in enumerate((-0.5 * (ux * lx + uy * ly), ux, uy, -0.5 * ca, -cb, -0.5 * cc)):
        for term_at, term in enumerate(split(value, 3)):
            scatter_rows(coefs, 8 * term_at + at, 32, term)
    for k in range(3):
        terms = split(feature(6 + k), 3)
        for at, term_at in enumerate((0, 1, 0, 1, 2, 0)):
            scatter_rows(colours, 3 * at + k, 32, terms[term_at])

    def render(j):
        rows = pl.ds(pl.multiple_of(j * 32, 32), 32)
        power = dot(basis_pe, take_rows(coefs, rows).astype(BF16))
        alpha = live_op[pl.ds(j, 1), :] * jnp.exp(power)
        keep = 1.0 - alpha
        hi, lo = two(jnp.log(keep))
        weight = alpha * jnp.exp(dot(hi, before) + dot(lo, before))
        hi, lo = two(weight)
        colour = take_rows(colours, rows).astype(BF16)
        image = dot_nt(colour, hi) + dot_nt(colour, lo)
        for k in range(3):
            rendered[0, k, pl.ds(j, 1), :] = (
                image[k : k + 1] + image[k + 3 : k + 4] + image[k + 12 : k + 13]
            )
        tint = dot(cots[j], hi) + dot(cots[j], lo)
        scatter_rows(tints, j, tiles_here, tint[0:3] + tint[6:9] + tint[15:18])
        pulled = dot(cots_t[j], colour) * weight
        hi, lo = two(pulled)
        later = dot(hi, after) + dot(lo, after)
        rough = pl.reciprocal(keep, approx=True)
        hi, lo = two(pulled - later * (alpha * (rough * (2.0 - keep * rough))))
        moment = dot(basis_ep, hi) + dot(basis_ep, lo)
        scatter_rows(moments, j, tiles_here, moment[0:8])

    step = 2 if tiles_here % 2 == 0 else 1

    @pl.loop(0, tiles_here // step)
    def _(at):
        for more in range(step):
            render(at * step + more)

    def moment(at):
        return take_rows(moments, slice(at * tiles_here, (at + 1) * tiles_here))

    m0, mx, my = moment(0), moment(1), moment(2)
    nx, ny = mx - lx * m0, my - ly * m0
    nxx = moment(3) - 2.0 * lx * mx + lx * lx * m0
    nxy = moment(4) - lx * my - ly * mx + lx * ly * m0
    nyy = moment(5) - 2.0 * ly * my + ly * ly * m0
    grads[...] = jnp.zeros_like(grads)
    for at, value in enumerate(
        (ca * nx + cb * ny, cc * ny + cb * nx, -0.5 * nxx, -nxy, -0.5 * nyy, m0 / op)
    ):
        scatter_rows(grads, at, 16, value)
    for k in range(3):
        scatter_rows(
            grads, 6 + k, 16, take_rows(tints, slice(k * tiles_here, (k + 1) * tiles_here))
        )
    back = 0.0
    for j in range(tiles_here):
        hi, lo = split(take_rows(grads, slice(16 * j, 16 * (j + 1))), 2)
        group = lists[j : j + 1, :] // LANES
        spread = [
            jnp.where(group == h, term, 0.0) for h in range(groups) for term in (hi, lo)
        ]
        back = back + dot_nt(jnp.concatenate(spread, axis=0).astype(BF16), low[j])
    slot_rows = [back[32 * h : 32 * h + 16] + back[32 * h + 16 : 32 * h + 32] for h in range(groups)]

    g = [
        jnp.concatenate([rows[at : at + 1] for rows in slot_rows], axis=0) for at in range(NFEAT)
    ]
    f = [by_slot[pl.ds(at, groups, stride=NSENT), :] for at in range(NSENT)]
    c = [cams[my_img, at] for at in range(10)]
    v0, v1, _ = conic(c, f[12:18])
    h = cov_grad((f[2], f[3], f[4]), (g[2], g[3], g[4]))
    shares = [g[0] * f[9 + a] + 2.0 * (h[0] * v0[a] + h[1] * v1[a]) for a in range(3)]
    shares += [g[1] * f[9 + a] + 2.0 * (h[2] * v1[a] + h[1] * v0[a]) for a in range(3)]
    shares += [g[0], g[1]]
    shares += [sum(g[6 + k] * f[18 + 3 * d + k] for k in range(3)) for d in range(2)]
    slot_lane = lax.rem(lax.broadcasted_iota(jnp.int32, (16, LANES), 1), cap)
    is_camera = lax.broadcasted_iota(jnp.int32, (16, LANES), 0) == NFEAT
    camera_row = jnp.zeros((1, LANES), F32)
    for at, share in enumerate(shares):
        total = jnp.sum(jnp.sum(share, axis=0, keepdims=True), axis=1, keepdims=True)
        camera_row = jnp.where(slot_lane[0:1] == at, total, camera_row)
    for at, rows in enumerate(slot_rows):
        slots[at * LANES : (at + 1) * LANES, 0:NBACK] = jnp.transpose(
            jnp.where(is_camera, camera_row, rows)
        )
    grad_send[...] = jnp.concatenate(
        [slots[pl.ds(c, devices, stride=cap), 0:NBACK] for c in range(cap)], axis=1
    ).reshape(devices, 1, cap * NBACK)
    returning = exchange(2, grad_send, grad_recv)
    sent(1, feat_send)
    arrive(2, grad_recv, returning)
    back_out[...] = grad_recv[...].reshape(devices, cap * NBACK)
    sent(2, grad_send)


def owner_kernel(
    sizes,
    means,
    log_scales,
    quat_w,
    quat_v,
    opacity,
    cams,
    back,
    asked,
    harm,
    rendered_in,
    rendered,
    param_grad,
    camera_grad,
    dense,
    slots,
    result,
):
    n_img, n_tile, cap = sizes
    owned = means.shape[1]
    high = owned // LANES
    devices = n_img * n_tile
    per_img = n_tile * cap
    rendered[...] = rendered_in[...]
    load_dense((means, log_scales, quat_w, quat_v, opacity), dense)

    def row(at):
        return dense[at * high : (at + 1) * high, :]

    quat, inverse, rot, squares, sigma = geometry(row)
    base = 1.0 / (1.0 + jnp.exp(-row(10)))
    packed = back[...]
    for c in range(cap):
        slots[pl.ds(c, devices, stride=cap), 0:NBACK] = packed[:, c * NBACK : (c + 1) * NBACK]
    g_mean = [0.0, 0.0, 0.0]
    g_base = 0.0
    g_sigma = [[0.0] * 3 for _ in range(3)]
    g_colour = []
    for i in range(n_img):
        mine = jnp.concatenate(
            [
                jnp.transpose(slots[at : at + LANES, :])[0:NBACK]
                for at in range(i * per_img, (i + 1) * per_img, LANES)
            ],
            axis=1,
        )
        fold = mine[NFEAT : NFEAT + 1, 0:LANES]
        for at in range(LANES, per_img, LANES):
            fold = fold + mine[NFEAT : NFEAT + 1, at : at + LANES]
        shift = LANES // 2
        while shift >= cap:
            fold = fold + pltpu.roll(fold, shift, 1)
            shift //= 2
        camera_grad[i : i + 1, :] = fold[:, 0:10]
        lanes = slice(i * per_img, (i + 1) * per_img)
        pick = mask_of(asked[0:1, lanes], high)
        low = as_bf16(mask_of(asked[1:2, lanes], LANES))
        spread = jnp.concatenate(
            [
                jnp.concatenate(
                    [jnp.where(pick, term[at : at + 1], 0.0) for at in range(NFEAT)], axis=0
                ).astype(BF16)
                for term in split(mine, 2)
            ],
            axis=1,
        )
        full = dot_nt(spread, jnp.concatenate([low] * 2, axis=1))
        g = [full[at * high : (at + 1) * high] for at in range(NFEAT)]
        c = [cams[i, at] for at in range(8)]
        _, _, con = conic(c, sigma)
        h = cov_grad(con, (g[2], g[3], g[4]))
        for a in range(3):
            g_mean[a] = g_mean[a] + c[a] * g[0] + c[3 + a] * g[1]
            for b in range(a, 3):
                g_sigma[a][b] = (
                    g_sigma[a][b]
                    + (c[a] * c[b]) * h[0]
                    + (c[a] * c[3 + b] + c[3 + a] * c[b]) * h[1]
                    + (c[3 + a] * c[3 + b]) * h[2]
                )
        g_base = g_base + g[5]
        g_colour.append(g[6:9])

    def put(at, value):
        result[at * high : (at + 1) * high, :] = value

    for k in range(3):
        for m in range(16):
            put(
                11 + 16 * k + m,
                sum(harm[i, m : m + 1, :] * g_colour[i][k] for i in range(n_img)),
            )
    for a in range(3):
        put(a, g_mean[a])
        for b in range(a):
            g_sigma[a][b] = g_sigma[b][a]
    r = [[None] * 3 for _ in range(3)]
    for b in range(3):
        pull = [
            g_sigma[a][0] * rot[0][b] + g_sigma[a][1] * rot[1][b] + g_sigma[a][2] * rot[2][b]
            for a in range(3)
        ]
        twice = 2.0 * squares[b]
        for a in range(3):
            r[a][b] = twice * pull[a]
        put(3 + b, r[0][b] * rot[0][b] + r[1][b] * rot[1][b] + r[2][b] * rot[2][b])
    w, x, y, z = quat
    g_quat = (
        z * (r[1][0] - r[0][1]) + y * (r[0][2] - r[2][0]) + x * (r[2][1] - r[1][2]),
        y * (r[0][1] + r[1][0])
        + z * (r[0][2] + r[2][0])
        + w * (r[2][1] - r[1][2])
        - 2.0 * x * (r[1][1] + r[2][2]),
        x * (r[0][1] + r[1][0])
        + z * (r[1][2] + r[2][1])
        + w * (r[0][2] - r[2][0])
        - 2.0 * y * (r[0][0] + r[2][2]),
        x * (r[0][2] + r[2][0])
        + y * (r[1][2] + r[2][1])
        + w * (r[1][0] - r[0][1])
        - 2.0 * z * (r[0][0] + r[1][1]),
    )
    along = sum(quat[a] * g_quat[a] for a in range(4))
    for a in range(4):
        put(6 + a, 2.0 * (g_quat[a] - quat[a] * along) * inverse)
    put(10, g_base * base * (1.0 - base))
    rows = param_grad.shape[0]
    for h in range(high):
        param_grad[:, h * LANES : (h + 1) * LANES] = result[pl.ds(h, rows, stride=high), :]


def local(
    means,
    log_scales,
    quat_w,
    quat_v,
    opacity,
    sh_coeffs,
    cameras,
    requests,
    lists,
    counts,
    image_cot,
):
    n_img, n_tile, cap = requests.shape[2:]
    devices = n_img * n_tile
    n_slots = devices * cap
    owned = means.shape[1]
    high = owned // LANES
    tiles_here, length = lists.shape[1:]
    pix = image_cot.shape[3]
    vmem = pl.BlockSpec(memory_space=pltpu.VMEM)
    smem = pl.BlockSpec(memory_space=pltpu.SMEM)
    small = (means, log_scales, quat_w, quat_v, opacity)
    few = sum(part.shape[0] for part in small)
    rows = few + sh_coeffs.shape[0]
    image_shape = jax.ShapeDtypeStruct(image_cot.shape, F32)
    rendered, back, asked, harm = pl.pallas_call(
        functools.partial(render_kernel, (n_img, n_tile, cap, tiles_here, length, pix)),
        out_shape=(
            image_shape,
            jax.ShapeDtypeStruct((devices, cap * NBACK), F32),
            jax.ShapeDtypeStruct((2, n_slots), jnp.int32),
            jax.ShapeDtypeStruct((n_img, 16, LANES), F32),
        ),
        in_specs=[vmem] * 6 + [smem, vmem, vmem, smem, vmem],
        out_specs=(vmem,) * 4,
        scratch_shapes=[
            pltpu.VMEM((devices, 1, cap), jnp.int32),
            pltpu.VMEM((devices, 1, cap * NSENT), F32),
            pltpu.VMEM((devices, 1, cap * NSENT), F32),
            pltpu.VMEM((devices, 1, cap * NBACK), F32),
            pltpu.VMEM((devices, 1, cap * NBACK), F32),
            pltpu.VMEM((rows * high + high, LANES), F32),
            pltpu.VMEM((high * NSENT + NSENT, LANES), F32),
            pltpu.VMEM((n_img, high * NSENT, 3 * LANES), BF16),
            pltpu.VMEM((n_slots + cap, LANES), F32),
            pltpu.VMEM((n_slots // LANES * NSENT + NSENT, LANES), F32),
            pltpu.VMEM((tiles_here, LANES, length), BF16),
            pltpu.VMEM((length // LANES, 16 * tiles_here + 16, LANES), F32),
            pltpu.VMEM((length // LANES, 32 * tiles_here + 32, LANES), F32),
            pltpu.VMEM((length // LANES, 32 * tiles_here + 32, LANES), F32),
            pltpu.VMEM((tiles_here, 32, pix), BF16),
            pltpu.VMEM((tiles_here, pix, 32), BF16),
            pltpu.VMEM((tiles_here, length), F32),
            pltpu.VMEM((length // LANES, 9 * tiles_here, LANES), F32),
            pltpu.VMEM((length // LANES, 4 * tiles_here, LANES), F32),
            pltpu.VMEM((length // LANES, 16 * tiles_here + 16, LANES), F32),
            pltpu.VMEM((n_img, 3, 16, LANES), F32),
            pltpu.SemaphoreType.DMA((3,)),
            pltpu.SemaphoreType.DMA((3,)),
            pltpu.SemaphoreType.DMA((3,)),
        ],
        compiler_params=pltpu.CompilerParams(
            collective_id=0, has_side_effects=True, vmem_limit_bytes=48 * 1024 * 1024
        ),
    )(
        *small,
        sh_coeffs,
        cameras,
        requests.reshape(devices, 1, cap),
        lists[0],
        counts,
        image_cot,
    )
    return pl.pallas_call(
        functools.partial(owner_kernel, (n_img, n_tile, cap)),
        out_shape=(
            image_shape,
            jax.ShapeDtypeStruct((rows, owned), F32),
            jax.ShapeDtypeStruct(cameras.shape, F32),
        ),
        in_specs=[vmem] * 5 + [smem] + [vmem] * 4,
        out_specs=(vmem,) * 3,
        scratch_shapes=[
            pltpu.VMEM((few * high + high, LANES), F32),
            pltpu.VMEM((n_slots + cap, LANES), F32),
            pltpu.VMEM((rows * high + high, LANES), F32),
        ],
        compiler_params=pltpu.CompilerParams(vmem_limit_bytes=16 * 1024 * 1024),
    )(*small, cameras, back, asked, harm, rendered)


def solution(mesh):
    owners = P(None, ("img", "tile"))
    images = P("img", None, "tile", None)
    return jax.shard_map(
        local,
        mesh=mesh,
        in_specs=(owners,) * 6
        + (P(), P("img", "tile", None, None, None), P("img", "tile", None), P("img", "tile"), images),
        out_specs=(images, owners, P()),
        check_vma=False,
    )
```

profile of v0, /device:TPU:0, one launch (start us, length us, event | category | flops | bytes accessed | tf_op | source)
XLA Modules:
  0.0 39.8 jit_solution(7335481421471729531)
XLA Ops:
  0.6 0.0 copy-start.9
  0.6 0.0 copy-start.10
  0.7 0.7 %copy-done.9 = f32[2,10]{1,0:T(2,128)S(1)} copy-done((f32[2,10]{1,0:T(2,128)S(1)}, f32[2,10]{1,0:T(2,128)}, u32[]{:S(2)}) %copy-start.9) | copy-done | bytes 104
  1.3 0.0 copy-done.10
  1.3 0.0 copy-start
  1.3 1.0 %copy-done = f32[48,2048]{1,0:T(8,128)S(1)} copy-done((f32[48,2048]{1,0:T(8,128)S(1)}, f32[48,2048]{1,0:T(8,128)}, u32[]{:S(2)}) %copy-start) | copy-done | bytes 393240
  2.3 0.0 copy-start.1
  2.3 0.8 %copy-done.1 = f32[3,2048]{1,0:T(4,128)S(1)} copy-done((f32[3,2048]{1,0:T(4,128)S(1)}, f32[3,2048]{1,0:T(4,128)}, u32[]{:S(2)}) %copy-start.1) | copy-done | bytes 24600
  3.1 0.0 copy-start.2
  3.1 0.8 %copy-done.2 = f32[3,2048]{1,0:T(4,128)S(1)} copy-done((f32[3,2048]{1,0:T(4,128)S(1)}, f32[3,2048]{1,0:T(4,128)}, u32[]{:S(2)}) %copy-start.2) | copy-done | bytes 24600
  3.8 0.0 copy-start.3
  3.8 0.8 %copy-done.3 = f32[3,2048]{1,0:T(4,128)S(1)} copy-done((f32[3,2048]{1,0:T(4,128)S(1)}, f32[3,2048]{1,0:T(4,128)}, u32[]{:S(2)}) %copy-start.3) | copy-done | bytes 24600
  4.6 0.0 copy-start.4
  4.6 0.7 %copy-done.4 = f32[1,2048]{1,0:T(1,128)S(1)} copy-done((f32[1,2048]{1,0:T(1,128)S(1)}, f32[1,2048]{1,0:T(1,128)}, u32[]{:S(2)}) %copy-start.4) | copy-done | bytes 8216
  5.3 0.0 copy-start.5
  5.3 0.7 %copy-done.5 = f32[1,2048]{1,0:T(1,128)S(1)} copy-done((f32[1,2048]{1,0:T(1,128)S(1)}, f32[1,2048]{1,0:T(1,128)}, u32[]{:S(2)}) %copy-start.5) | copy-done | bytes 8216
  6.0 0.0 copy-start.6
  6.0 0.7 %copy-done.6 = f32[1,3,8,256]{3,2,1,0:T(8,128)S(1)} copy-done((f32[1,3,8,256]{3,2,1,0:T(8,128)S(1)}, f32[1,3,8,256]{3,2,1,0:T(8,128)}, u32[]{:S(2)}) %copy-start.6) | copy-done | bytes 24600
  6.7 0.0 copy-start.7
  6.7 0.7 %copy-done.7 = s32[1,1,2,16,16]{4,3,2,1,0:T(8,128)S(1)} copy-done((s32[1,1,2,16,16]{4,3,2,1,0:T(8,128)S(1)}, s32[1,1,2,16,16]{4,3,2,1,0:T(8,128)}, u32[]{:S(2)}) %copy-start.7) | copy-done | bytes 2072
  7.4 0.0 copy-start.8
  7.4 0.7 %copy-done.8 = s32[1,8,256]{2,1,0:T(8,128)S(1)} copy-done((s32[1,8,256]{2,1,0:T(8,128)S(1)}, s32[1,8,256]{2,1,0:T(8,128)}, u32[]{:S(2)}) %copy-start.8) | copy-done | bytes 8216
  8.1 29.6 %shard_map.130 = (f32[1,3,8,256]{3,2,1,0:T(8,128)S(1)}, f32[32,256]{1,0:T(8,128)S(1)}, s32[2,512]{1,0:T(2,128)S(1)}, f32[2,16,128]{2,1,0:T(8,128)S(1)}) custom-call(f32[3,2048]{1,0:T(4,128)S(1)} %copy-done.1, f32[3,2048]{1,0:T(4,128)S(1)} %copy-done.2, f32[1,2048]{1,0:T(1,128)S(1)} %copy-done.4, f32[3,2048]{1,0:T(4,128)S(1)} %copy-done.3, ...), custom_call_target="tpu_custom_call" | custom-call | tf_op jit(solution)/shard_map/pallas_call | solution.py:743
  37.8 2.0 %shard_map.131 = (f32[1,3,8,256]{3,2,1,0:T(8,128)}, f32[59,2048]{1,0:T(8,128)}, f32[2,10]{1,0:T(2,128)}) custom-call(f32[3,2048]{1,0:T(4,128)S(1)} %copy-done.1, f32[3,2048]{1,0:T(4,128)S(1)} %copy-done.2, f32[1,2048]{1,0:T(1,128)S(1)} %copy-done.4, f32[3,2048]{1,0:T(4,128)S(1)} %copy-done.3, f32[1,2048]{1,0:T(1,128)S(1)} %copy-done.5, ...), custom_call_target="tpu_custom_call" | custom-call | tf_op jit(solution)/shard_map/pallas_call | solution.py:791
Async XLA Ops:
  0.6 0.7 %copy-start.9 = (f32[2,10]{1,0:T(2,128)S(1)}, f32[2,10]{1,0:T(2,128)}, u32[]{:S(2)}) copy-start(f32[2,10]{1,0:T(2,128)} %cams.3) | copy-start | bytes 244
  0.6 0.7 %copy-start.10 = (s32[1,8]{1,0:T(1,128)S(1)}, s32[1,8]{1,0:T(1,128)}, u32[]{:S(2)}) copy-start(s32[1,8]{1,0:T(1,128)} %counts.1) | copy-start | bytes 100
  1.3 1.0 %copy-start = (f32[48,2048]{1,0:T(8,128)S(1)}, f32[48,2048]{1,0:T(8,128)}, u32[]{:S(2)}) copy-start(f32[48,2048]{1,0:T(8,128)} %sh.1) | copy-start | bytes 1179652
  2.3 0.8 %copy-start.1 = (f32[3,2048]{1,0:T(4,128)S(1)}, f32[3,2048]{1,0:T(4,128)}, u32[]{:S(2)}) copy-start(f32[3,2048]{1,0:T(4,128)} %means.3) | copy-start | bytes 73732
  3.1 0.8 %copy-start.2 = (f32[3,2048]{1,0:T(4,128)S(1)}, f32[3,2048]{1,0:T(4,128)}, u32[]{:S(2)}) copy-start(f32[3,2048]{1,0:T(4,128)} %log_scales.3) | copy-start | bytes 73732
  3.8 0.8 %copy-start.3 = (f32[3,2048]{1,0:T(4,128)S(1)}, f32[3,2048]{1,0:T(4,128)}, u32[]{:S(2)}) copy-start(f32[3,2048]{1,0:T(4,128)} %quat_v.3) | copy-start | bytes 73732
  4.6 0.7 %copy-start.4 = (f32[1,2048]{1,0:T(1,128)S(1)}, f32[1,2048]{1,0:T(1,128)}, u32[]{:S(2)}) copy-start(f32[1,2048]{1,0:T(1,128)} %quat_w.3) | copy-start | bytes 24580
  5.3 0.7 %copy-start.5 = (f32[1,2048]{1,0:T(1,128)S(1)}, f32[1,2048]{1,0:T(1,128)}, u32[]{:S(2)}) copy-start(f32[1,2048]{1,0:T(1,128)} %opacity.3) | copy-start | bytes 24580
  6.0 0.7 %copy-start.6 = (f32[1,3,8,256]{3,2,1,0:T(8,128)S(1)}, f32[1,3,8,256]{3,2,1,0:T(8,128)}, u32[]{:S(2)}) copy-start(f32[1,3,8,256]{3,2,1,0:T(8,128)} %cot.1) | copy-start | bytes 73732
  6.7 0.7 %copy-start.7 = (s32[1,1,2,16,16]{4,3,2,1,0:T(8,128)S(1)}, s32[1,1,2,16,16]{4,3,2,1,0:T(8,128)}, u32[]{:S(2)}) copy-start(s32[1,1,2,16,16]{4,3,2,1,0:T(8,128)} %param.18) | copy-start | bytes 6148
  7.4 0.7 %copy-start.8 = (s32[1,8,256]{2,1,0:T(8,128)S(1)}, s32[1,8,256]{2,1,0:T(8,128)}, u32[]{:S(2)}) copy-start(s32[1,8,256]{2,1,0:T(8,128)} %param.19) | copy-start | bytes 24580
where the time goes:
time: 40.4 us; the launch traced here: 39.8 us
  Pallas kernels  31.6 us (78%)
  local copies, waits for them, and re-layouts  7.48 us (19%)
  between operations  0.67 us (2%)
    pallas_call x1, Pallas kernels, local(): pl.pallas_call(functools.partial(render_kernel, (n_img, n_tile, cap, tile...  29.6 us
    unnamed x22, local copies, waits for them, and re-layouts  7.48 us
    pallas_call x1, Pallas kernels, local(): pl.pallas_call(functools.partial(owner_kernel, (n_img, n_tile, cap)), out...  2.01 us

commit v1 on v0

--- a/solution.py
+++ b/solution.py
@@ -236,21 +236,30 @@
 
 def render_kernel(
     sizes,
+    means_hbm,
+    log_scales_hbm,
+    quat_w_hbm,
+    quat_v_hbm,
+    opacity_hbm,
+    sh_hbm,
+    cams,
+    requests,
+    lists_hbm,
+    counts,
+    cot_hbm,
+    rendered,
+    back_out,
+    ask_out,
+    harm_out,
     means,
     log_scales,
     quat_w,
     quat_v,
     opacity,
     sh,
-    cams,
-    requests,
     lists,
-    counts,
     cot,
-    rendered,
-    back_out,
-    ask_out,
-    harm_out,
+    in_sem,
     ask_recv,
     feat_send,
     feat_recv,
@@ -291,6 +300,24 @@
         other = lax.rem(me + k, devices)
         return other, (other // n_tile, lax.rem(other, n_tile))
 
+    loads = [
+        pltpu.make_async_copy(source, target, in_sem.at[at])
+        for at, (source, target) in enumerate(
+            (
+                (means_hbm, means),
+                (log_scales_hbm, log_scales),
+                (quat_w_hbm, quat_w),
+                (quat_v_hbm, quat_v),
+                (opacity_hbm, opacity),
+                (sh_hbm, sh),
+                (lists_hbm, lists),
+                (cot_hbm, cot),
+            )
+        )
+    ]
+    for load in loads:
+        load.start()
+
     barrier = pltpu.get_barrier_semaphore()
 
     @pl.loop(1, devices)
@@ -324,27 +351,29 @@
         others = source.at[pl.ds(0, devices - 1)]
         pltpu.make_async_copy(others, others, send_sem.at[at]).wait()
 
+    cam = [[cams[i, c] for c in range(10)] for i in range(n_img)]
+    img_rows = -(-n_img // 8) * 8
+    img_row = lax.broadcasted_iota(jnp.int32, (img_rows, LANES), 0)
+    polar = jnp.zeros((img_rows, LANES), F32)
+    azimuth = jnp.zeros((img_rows, LANES), F32)
+    for i in range(n_img):
+        polar = jnp.where(img_row == i, cam[i][8], polar)
+        azimuth = jnp.where(img_row == i, cam[i][9], azimuth)
+    sp, cp = jnp.sin(polar), jnp.cos(polar)
+    sz, cz = jnp.sin(azimuth), jnp.cos(azimuth)
+    values, by_x, by_y, by_z = harmonics(sp * cz, sp * sz, cp)
+    for m in range(16):
+        by_polar = by_x[m] * (cp * cz) + by_y[m] * (cp * sz) - by_z[m] * sp
+        by_azimuth = by_y[m] * (sp * cz) - by_x[m] * (sp * sz)
+        for i in range(n_img):
+            harm[i, 0, m : m + 1, :] = values[m][i : i + 1]
+            harm[i, 1, m : m + 1, :] = by_polar[i : i + 1]
+            harm[i, 2, m : m + 1, :] = by_azimuth[i : i + 1]
+    for i in range(n_img):
+        harm_out[i] = harm[i, 0]
+    for load in loads[:6]:
+        load.wait()
     load_dense((means, log_scales, quat_w, quat_v, opacity, sh), dense)
-    cam = [[cams[i, c] for c in range(10)] for i in range(n_img)]
-    row16 = lax.broadcasted_iota(jnp.int32, (16, LANES), 0)
-    for i in range(n_img):
-        polar = jnp.full((16, LANES), cam[i][8], F32)
-        azimuth = jnp.full((16, LANES), cam[i][9], F32)
-        sp, cp = jnp.sin(polar), jnp.cos(polar)
-        sz, cz = jnp.sin(azimuth), jnp.cos(azimuth)
-        values, by_x, by_y, by_z = harmonics(sp * cz, sp * sz, cp)
-        y_col = jnp.zeros((16, LANES), F32)
-        p_col = jnp.zeros((16, LANES), F32)
-        z_col = jnp.zeros((16, LANES), F32)
-        for m in range(16):
-            here = row16 == m
-            y_col = jnp.where(here, values[m], y_col)
-            p_col = jnp.where(here, by_x[m] * cp * cz + by_y[m] * cp * sz - by_z[m] * sp, p_col)
-            z_col = jnp.where(here, -by_x[m] * sp * sz + by_y[m] * sp * cz, z_col)
-        harm[i, 0] = y_col
-        harm[i, 1] = p_col
-        harm[i, 2] = z_col
-        harm_out[i] = y_col
 
     pl.semaphore_wait(barrier, devices - 1)
     asking = exchange(0, requests, ask_recv)
@@ -379,6 +408,8 @@
         for at, term in enumerate(split(project[0 : high * NSENT, :], 3)):
             feats[i, :, at * LANES : (at + 1) * LANES] = term.astype(BF16)
 
+    for load in loads[6:]:
+        load.wait()
     coefs[...] = jnp.zeros_like(coefs)
     colours[...] = jnp.zeros_like(colours)
     for j in range(tiles_here):
@@ -446,7 +477,7 @@
         [slots[pl.ds(c, devices, stride=cap), 0:NSENT] for c in range(cap)], axis=1
     ).reshape(devices, 1, cap * NSENT)
     sending = exchange(1, feat_send, feat_recv)
-    sent(0, ask_recv)
+    sent(0, requests)
     arrive(1, feat_recv, sending)
     packed = feat_recv[...].reshape(devices, cap * NSENT)
     for c in range(cap):
@@ -736,6 +767,7 @@
     pix = image_cot.shape[3]
     vmem = pl.BlockSpec(memory_space=pltpu.VMEM)
     smem = pl.BlockSpec(memory_space=pltpu.SMEM)
+    hbm = pl.BlockSpec(memory_space=pl.ANY)
     small = (means, log_scales, quat_w, quat_v, opacity)
     few = sum(part.shape[0] for part in small)
     rows = few + sh_coeffs.shape[0]
@@ -748,9 +780,13 @@
             jax.ShapeDtypeStruct((2, n_slots), jnp.int32),
             jax.ShapeDtypeStruct((n_img, 16, LANES), F32),
         ),
-        in_specs=[vmem] * 6 + [smem, vmem, vmem, smem, vmem],
+        in_specs=[hbm] * 6 + [smem, hbm, hbm, smem, hbm],
         out_specs=(vmem,) * 4,
         scratch_shapes=[
+            *(pltpu.VMEM(part.shape, F32) for part in (*small, sh_coeffs)),
+            pltpu.VMEM((tiles_here, length), jnp.int32),
+            pltpu.VMEM(image_cot.shape, F32),
+            pltpu.SemaphoreType.DMA((8,)),
             pltpu.VMEM((devices, 1, cap), jnp.int32),
             pltpu.VMEM((devices, 1, cap * NSENT), F32),
             pltpu.VMEM((devices, 1, cap * NSENT), F32),
@@ -777,7 +813,7 @@
             pltpu.SemaphoreType.DMA((3,)),
         ],
         compiler_params=pltpu.CompilerParams(
-            collective_id=0, has_side_effects=True, vmem_limit_bytes=48 * 1024 * 1024
+            collective_id=0, has_side_effects=True, vmem_limit_bytes=60 * 1024 * 1024
         ),
     )(
         *small,
@@ -802,7 +838,7 @@
             pltpu.VMEM((n_slots + cap, LANES), F32),
             pltpu.VMEM((rows * high + high, LANES), F32),
         ],
-        compiler_params=pltpu.CompilerParams(vmem_limit_bytes=16 * 1024 * 1024),
+        compiler_params=pltpu.CompilerParams(vmem_limit_bytes=60 * 1024 * 1024),
     )(*small, cameras, back, asked, harm, rendered)
 
 

time: 40.4 us -> 34 us (0.84)
  local copies, waits for them, and re-layouts: 7.48 us -> 0 us
  Pallas kernels: 31.6 us -> 33.1 us
    unnamed x22 -> x0, local copies, waits for them, and re-layouts: 7.48 us -> none
    pallas_call x1, Pallas kernels: 29.6 us -> 30.8 us  [local(): pl.pallas_call(functools.partial(render_kernel, (n_img, n_tile, cap, tile...]
where the time goes in v1:
time: 34 us; the launch traced here: 33.7 us
  Pallas kernels  33.1 us (97%)
  between operations  0.64 us (2%)
    pallas_call x1, Pallas kernels, local(): pl.pallas_call(functools.partial(render_kernel, (n_img, n_tile, cap, tile...  30.8 us
    pallas_call x1, Pallas kernels, local(): pl.pallas_call(functools.partial(owner_kernel, (n_img, n_tile, cap)), out...  2.32 us

profile of v1, /device:TPU:0, one launch (start us, length us, event | category | flops | bytes accessed | tf_op | source)
XLA Modules:
  0.0 33.7 jit_solution(397843950370039288)
XLA Ops:
  0.6 30.8 %shard_map.130 = (f32[1,3,8,256]{3,2,1,0:T(8,128)}, f32[32,256]{1,0:T(8,128)}, s32[2,512]{1,0:T(2,128)}, f32[2,16,128]{2,1,0:T(8,128)}) custom-call(f32[3,2048]{1,0:T(4,128)} %means.1, f32[3,2048]{1,0:T(4,128)} %log_scales.1, f32[1,2048]{1,0:T(1,128)} %quat_w.1, f32[3,2048]{1,0:T(4,128)} %quat_v.1, f32[1,2048]{1,0:T(1,128)} %opacity.1, f32[48,2048]{1,0:T(8,128)} %sh_hbm.1, ...), custom_call_target="tpu_custom_call" | custom-call | tf_op jit(solution)/shard_map/pallas_call | solution.py:775
  31.4 2.3 %shard_map.131 = (f32[1,3,8,256]{3,2,1,0:T(8,128)}, f32[59,2048]{1,0:T(8,128)}, f32[2,10]{1,0:T(2,128)}) custom-call(f32[3,2048]{1,0:T(4,128)} %means.1, f32[3,2048]{1,0:T(4,128)} %log_scales.1, f32[1,2048]{1,0:T(1,128)} %quat_w.1, f32[3,2048]{1,0:T(4,128)} %quat_v.1, f32[1,2048]{1,0:T(1,128)} %opacity.1, f32[2,10]{1,0:T(2,128)} %cams.3, ...), custom_call_target="tpu_custom_call" | custom-call | tf_op jit(solution)/shard_map/pallas_call | solution.py:827

commit v2 on v1

--- a/solution.py
+++ b/solution.py
@@ -280,6 +280,8 @@
     moments,
     tints,
     grads,
+    tinted,
+    pictures,
     harm,
     send_sem,
     recv_sem,
@@ -473,11 +475,35 @@
         for h in range(1, high):
             total = total + got[h * NSENT : (h + 1) * NSENT] * pick[h : h + 1]
         slots[lanes, 0:NSENT] = jnp.transpose(total)
-    feat_send[...] = jnp.concatenate(
-        [slots[pl.ds(c, devices, stride=cap), 0:NSENT] for c in range(cap)], axis=1
-    ).reshape(devices, 1, cap * NSENT)
-    sending = exchange(1, feat_send, feat_recv)
+        feat_send[i * n_tile : (i + 1) * n_tile] = jnp.concatenate(
+            [
+                slots[pl.ds(i * per_img + c, n_tile, stride=cap), 0:NSENT]
+                for c in range(cap)
+            ],
+            axis=1,
+        ).reshape(n_tile, 1, cap * NSENT)
+
+        @pl.loop(0, n_tile)
+        def _(k):
+            place = lax.rem(my_tile + k, n_tile)
+            other = i * n_tile + place
+
+            @pl.when(other != me)
+            def _():
+                pltpu.make_async_remote_copy(
+                    src_ref=feat_send.at[other],
+                    dst_ref=feat_recv.at[me],
+                    send_sem=send_sem.at[1],
+                    recv_sem=recv_sem.at[1],
+                    device_id=(i, place),
+                    device_id_type=MESH,
+                ).start()
+
+    sending = pltpu.make_async_copy(feat_send.at[me], feat_recv.at[me], own_sem.at[1])
+    sending.start()
     sent(0, requests)
+    tinted[...] = jnp.zeros_like(tinted)
+    pictures[...] = jnp.zeros_like(pictures)
     arrive(1, feat_recv, sending)
     packed = feat_recv[...].reshape(devices, cap * NSENT)
     for c in range(cap):
@@ -523,37 +549,84 @@
         terms = split(feature(6 + k), 3)
         for at, term_at in enumerate((0, 1, 0, 1, 2, 0)):
             scatter_rows(colours, 3 * at + k, 32, terms[term_at])
-
-    def render(j):
-        rows = pl.ds(pl.multiple_of(j * 32, 32), 32)
-        power = dot(basis_pe, take_rows(coefs, rows).astype(BF16))
-        alpha = live_op[pl.ds(j, 1), :] * jnp.exp(power)
-        keep = 1.0 - alpha
-        hi, lo = two(jnp.log(keep))
-        weight = alpha * jnp.exp(dot(hi, before) + dot(lo, before))
-        hi, lo = two(weight)
-        colour = take_rows(colours, rows).astype(BF16)
-        image = dot_nt(colour, hi) + dot_nt(colour, lo)
-        for k in range(3):
-            rendered[0, k, pl.ds(j, 1), :] = (
-                image[k : k + 1] + image[k + 3 : k + 4] + image[k + 12 : k + 13]
-            )
-        tint = dot(cots[j], hi) + dot(cots[j], lo)
-        scatter_rows(tints, j, tiles_here, tint[0:3] + tint[6:9] + tint[15:18])
-        pulled = dot(cots_t[j], colour) * weight
-        hi, lo = two(pulled)
-        later = dot(hi, after) + dot(lo, after)
-        rough = pl.reciprocal(keep, approx=True)
-        hi, lo = two(pulled - later * (alpha * (rough * (2.0 - keep * rough))))
-        moment = dot(basis_ep, hi) + dot(basis_ep, lo)
-        scatter_rows(moments, j, tiles_here, moment[0:8])
+        for at in range(2):
+            scatter_rows(tinted, at * 4 * tiles_here + k, 4, terms[at])
+    painted = jnp.transpose(take_rows(tinted, slice(0, 8 * tiles_here)))
+    painted_lane = lax.rem(
+        lax.broadcasted_iota(jnp.int32, (length, 8 * tiles_here), 1), 4 * tiles_here
+    )
+
+    chunk = 64 if pix % 64 == 0 else pix
+    before2 = jnp.concatenate([before, before], axis=0)
+    after2 = jnp.concatenate([after, after], axis=0)
+    basis2 = jnp.concatenate([basis_ep, basis_ep], axis=1)
+
+    def chunks(function, *arrays):
+        parts = [
+            function(*(array[at : at + chunk] for array in arrays))
+            for at in range(0, pix, chunk)
+        ]
+        return tuple(jnp.concatenate(part, axis=0) for part in zip(*parts))
+
+    def render(tiles):
+        rows = [pl.ds(pl.multiple_of(j * 32, 32), 32) for j in tiles]
+        power = [dot(basis_pe, take_rows(coefs, r).astype(BF16)) for r in rows]
+        colour = [take_rows(colours, r).astype(BF16) for r in rows]
+        opacities = [live_op[pl.ds(j, 1), :] for j in tiles]
+        alpha, summed, weight, pair, pull, pulled, later = ([] for _ in range(7))
+        for at, j in enumerate(tiles):
+
+            def first_part(p, op_row=opacities[at]):
+                a = op_row * jnp.exp(p)
+                hi, lo = two(jnp.log(1.0 - a))
+                return a, jnp.concatenate([hi, lo], axis=1)
+
+            a, logs = chunks(first_part, power[at])
+            alpha.append(a)
+            summed.append(dot(logs, before2))
+            pull.append(dot(cots_t[j], colour[at]))
+        for at, j in enumerate(tiles):
+
+            def second_part(a, total, force):
+                w = a * jnp.exp(total)
+                p = force * w
+                return (*two(w), p, jnp.concatenate(two(p), axis=1))
+
+            hi, lo, p, wide = chunks(second_part, alpha[at], summed[at], pull[at])
+            pulled.append(p)
+            later.append(dot(wide, after2))
+            weight.append(jnp.concatenate([hi, lo], axis=0))
+            pair.append(jnp.concatenate([hi, lo], axis=1))
+        for at, j in enumerate(tiles):
+
+            def third_part(a, p, l):
+                keep = 1.0 - a
+                rough = pl.reciprocal(keep, approx=True)
+                return two(p - l * (a * (rough * (2.0 - keep * rough))))
+
+            hi, lo = chunks(third_part, alpha[at], pulled[at], later[at])
+            moment = dot(basis2, jnp.concatenate([hi, lo], axis=0))
+            scatter_rows(moments, j, tiles_here, moment[0:8])
+        picture = 0.0
+        for at, j in enumerate(tiles):
+            cot2 = jnp.concatenate([cots[j], cots[j]], axis=1)
+            tint = dot(cot2, weight[at])
+            scatter_rows(tints, j, tiles_here, tint[0:3] + tint[6:9] + tint[15:18])
+            brush = jnp.where(painted_lane // 4 == j, painted, 0.0).astype(BF16)
+            picture = picture + dot(pair[at], jnp.concatenate([brush, brush], axis=0))
+        pictures[...] += picture
 
     step = 2 if tiles_here % 2 == 0 else 1
 
     @pl.loop(0, tiles_here // step)
     def _(at):
-        for more in range(step):
-            render(at * step + more)
+        render([at * step + more for more in range(step)])
+
+    picture = jnp.transpose(pictures[...])
+    picture = picture[0 : 4 * tiles_here] + picture[4 * tiles_here : 8 * tiles_here]
+    for j in range(tiles_here):
+        for k in range(3):
+            rendered[0, k, j : j + 1, :] = picture[4 * j + k : 4 * j + k + 1]
 
     def moment(at):
         return take_rows(moments, slice(at * tiles_here, (at + 1) * tiles_here))
@@ -807,6 +880,8 @@
             pltpu.VMEM((length // LANES, 9 * tiles_here, LANES), F32),
             pltpu.VMEM((length // LANES, 4 * tiles_here, LANES), F32),
             pltpu.VMEM((length // LANES, 16 * tiles_here + 16, LANES), F32),
+            pltpu.VMEM((length // LANES, 8 * tiles_here + 4, LANES), F32),
+            pltpu.VMEM((pix, 8 * tiles_here), F32),
             pltpu.VMEM((n_img, 3, 16, LANES), F32),
             pltpu.SemaphoreType.DMA((3,)),
             pltpu.SemaphoreType.DMA((3,)),

time: 34 us -> 31.6 us (0.929)
  Pallas kernels: 33.1 us -> 30.7 us
    pallas_call x1, Pallas kernels: 30.8 us -> 28.4 us  [local(): pl.pallas_call(functools.partial(render_kernel, (n_img, n_tile, cap, tile...]
where the time goes in v2:
time: 31.6 us; the launch traced here: 31.4 us
  Pallas kernels  30.7 us (97%)
  between operations  0.64 us (2%)
    pallas_call x1, Pallas kernels, local(): pl.pallas_call(functools.partial(render_kernel, (n_img, n_tile, cap, tile...  28.4 us
    pallas_call x1, Pallas kernels, local(): pl.pallas_call(functools.partial(owner_kernel, (n_img, n_tile, cap)), out...  2.32 us

profile of v2, /device:TPU:0, one launch (start us, length us, event | category | flops | bytes accessed | tf_op | source)
XLA Modules:
  0.0 31.4 jit_solution(7366890235210427654)
XLA Ops:
  0.6 28.4 %shard_map.130 = (f32[1,3,8,256]{3,2,1,0:T(8,128)}, f32[32,256]{1,0:T(8,128)}, s32[2,512]{1,0:T(2,128)}, f32[2,16,128]{2,1,0:T(8,128)}) custom-call(f32[3,2048]{1,0:T(4,128)} %means.1, f32[3,2048]{1,0:T(4,128)} %log_scales.1, f32[1,2048]{1,0:T(1,128)} %quat_w.1, f32[3,2048]{1,0:T(4,128)} %quat_v.1, f32[1,2048]{1,0:T(1,128)} %opacity.1, f32[48,2048]{1,0:T(8,128)} %sh_hbm.1, ...), custom_call_target="tpu_custom_call" | custom-call | tf_op jit(solution)/shard_map/pallas_call | solution.py:848
  29.0 2.3 %shard_map.131 = (f32[1,3,8,256]{3,2,1,0:T(8,128)}, f32[59,2048]{1,0:T(8,128)}, f32[2,10]{1,0:T(2,128)}) custom-call(f32[3,2048]{1,0:T(4,128)} %means.1, f32[3,2048]{1,0:T(4,128)} %log_scales.1, f32[1,2048]{1,0:T(1,128)} %quat_w.1, f32[3,2048]{1,0:T(4,128)} %quat_v.1, f32[1,2048]{1,0:T(1,128)} %opacity.1, f32[2,10]{1,0:T(2,128)} %cams.3, ...), custom_call_target="tpu_custom_call" | custom-call | tf_op jit(solution)/shard_map/pallas_call | solution.py:902

commit v3 on v2

--- a/solution.py
+++ b/solution.py
@@ -322,7 +322,7 @@
 
     barrier = pltpu.get_barrier_semaphore()
 
-    @pl.loop(1, devices)
+    @pl.loop(1, devices, unroll=devices <= 32)
     def _(k):
         pl.semaphore_signal(barrier, inc=1, device_id=peer(k)[1], device_id_type=MESH)
 
@@ -330,7 +330,7 @@
         mine = pltpu.make_async_copy(source.at[me], target.at[me], own_sem.at[at])
         mine.start()
 
-        @pl.loop(1, devices)
+        @pl.loop(1, devices, unroll=devices <= 32)
         def _(k):
             other, where = peer(k)
             pltpu.make_async_remote_copy(
@@ -410,40 +410,6 @@
         for at, term in enumerate(split(project[0 : high * NSENT, :], 3)):
             feats[i, :, at * LANES : (at + 1) * LANES] = term.astype(BF16)
 
-    for load in loads[6:]:
-        load.wait()
-    coefs[...] = jnp.zeros_like(coefs)
-    colours[...] = jnp.zeros_like(colours)
-    for j in range(tiles_here):
-        low[j] = as_bf16(mask_of(jnp.bitwise_and(lists[j : j + 1, :], LANES - 1), LANES))
-        cot3 = jnp.concatenate([cot[0, k, j : j + 1, :] for k in range(3)], axis=0)
-        c1, c2, c3 = split(cot3, 3)
-        stack = jnp.concatenate([c1, c1, c2, c2, c1, c3, jnp.zeros((14, pix), F32)], axis=0)
-        cots[j] = stack.astype(BF16)
-        cots_t[j] = jnp.transpose(stack).astype(BF16)
-
-    def basis_of(pixel, which):
-        half = 0.5 * TILE_SIDE - 0.5
-        x = lax.rem(pixel, TILE_SIDE).astype(F32) - half
-        y = (pixel // TILE_SIDE).astype(F32) - half
-        out = jnp.where(which == 0, 1.0, 0.0)
-        for at, term in enumerate((x, y, x * x, x * y, y * y)):
-            out = jnp.where(which == at + 1, term, out)
-        return out.astype(BF16)
-
-    basis_pe = basis_of(
-        lax.broadcasted_iota(jnp.int32, (pix, 32), 0),
-        lax.rem(lax.broadcasted_iota(jnp.int32, (pix, 32), 1), 8),
-    )
-    basis_ep = basis_of(
-        lax.broadcasted_iota(jnp.int32, (16, pix), 1), lax.broadcasted_iota(jnp.int32, (16, pix), 0)
-    )
-    first = lax.broadcasted_iota(jnp.int32, (length, length), 0)
-    second = lax.broadcasted_iota(jnp.int32, (length, length), 1)
-    before = as_bf16(first < second)
-    after = as_bf16(first > second)
-    height = TILE_SIDE * tiles_here * n_tile / TW
-
     arrive(0, ask_recv, asking)
     asks = ask_recv[...].reshape(devices, cap)
     halves = jnp.concatenate(
@@ -483,7 +449,7 @@
             axis=1,
         ).reshape(n_tile, 1, cap * NSENT)
 
-        @pl.loop(0, n_tile)
+        @pl.loop(0, n_tile, unroll=n_tile <= 32)
         def _(k):
             place = lax.rem(my_tile + k, n_tile)
             other = i * n_tile + place
@@ -502,6 +468,41 @@
     sending = pltpu.make_async_copy(feat_send.at[me], feat_recv.at[me], own_sem.at[1])
     sending.start()
     sent(0, requests)
+
+    for load in loads[6:]:
+        load.wait()
+    coefs[...] = jnp.zeros_like(coefs)
+    colours[...] = jnp.zeros_like(colours)
+    for j in range(tiles_here):
+        low[j] = as_bf16(mask_of(jnp.bitwise_and(lists[j : j + 1, :], LANES - 1), LANES))
+        cot3 = jnp.concatenate([cot[0, k, j : j + 1, :] for k in range(3)], axis=0)
+        c1, c2, c3 = split(cot3, 3)
+        stack = jnp.concatenate([c1, c1, c2, c2, c1, c3, jnp.zeros((14, pix), F32)], axis=0)
+        cots[j] = stack.astype(BF16)
+        cots_t[j] = jnp.transpose(stack).astype(BF16)
+
+    def basis_of(pixel, which):
+        half = 0.5 * TILE_SIDE - 0.5
+        x = lax.rem(pixel, TILE_SIDE).astype(F32) - half
+        y = (pixel // TILE_SIDE).astype(F32) - half
+        out = jnp.where(which == 0, 1.0, 0.0)
+        for at, term in enumerate((x, y, x * x, x * y, y * y)):
+            out = jnp.where(which == at + 1, term, out)
+        return out.astype(BF16)
+
+    basis_pe = basis_of(
+        lax.broadcasted_iota(jnp.int32, (pix, 32), 0),
+        lax.rem(lax.broadcasted_iota(jnp.int32, (pix, 32), 1), 8),
+    )
+    basis_ep = basis_of(
+        lax.broadcasted_iota(jnp.int32, (16, pix), 1), lax.broadcasted_iota(jnp.int32, (16, pix), 0)
+    )
+    first = lax.broadcasted_iota(jnp.int32, (length, length), 0)
+    second = lax.broadcasted_iota(jnp.int32, (length, length), 1)
+    before = as_bf16(first < second)
+    after = as_bf16(first > second)
+    height = TILE_SIDE * tiles_here * n_tile / TW
+
     tinted[...] = jnp.zeros_like(tinted)
     pictures[...] = jnp.zeros_like(pictures)
     arrive(1, feat_recv, sending)
@@ -645,14 +646,18 @@
         scatter_rows(
             grads, 6 + k, 16, take_rows(tints, slice(k * tiles_here, (k + 1) * tiles_here))
         )
-    back = 0.0
+    spreads = []
     for j in range(tiles_here):
         hi, lo = split(take_rows(grads, slice(16 * j, 16 * (j + 1))), 2)
         group = lists[j : j + 1, :] // LANES
         spread = [
             jnp.where(group == h, term, 0.0) for h in range(groups) for term in (hi, lo)
         ]
-        back = back + dot_nt(jnp.concatenate(spread, axis=0).astype(BF16), low[j])
+        spreads.append(jnp.concatenate(spread, axis=0).astype(BF16))
+    back = dot_nt(
+        jnp.concatenate(spreads, axis=1),
+        jnp.concatenate([low[j] for j in range(tiles_here)], axis=1),
+    )
     slot_rows = [back[32 * h : 32 * h + 16] + back[32 * h + 16 : 32 * h + 32] for h in range(groups)]
 
     g = [

time: 31.6 us -> 31.1 us (0.984)
  Pallas kernels: 30.7 us -> 30.3 us
    pallas_call x1, Pallas kernels: 28.4 us -> 27.9 us  [local(): pl.pallas_call(functools.partial(render_kernel, (n_img, n_tile, cap, tile...]
where the time goes in v3:
time: 31.1 us; the launch traced here: 30.9 us
  Pallas kernels  30.3 us (97%)
  between operations  0.64 us (2%)
    pallas_call x1, Pallas kernels, local(): pl.pallas_call(functools.partial(render_kernel, (n_img, n_tile, cap, tile...  27.9 us
    pallas_call x1, Pallas kernels, local(): pl.pallas_call(functools.partial(owner_kernel, (n_img, n_tile, cap)), out...  2.33 us

profile of v3, /device:TPU:0, one launch (start us, length us, event | category | flops | bytes accessed | tf_op | source)
XLA Modules:
  0.0 30.9 jit_solution(17284660669424617140)
XLA Ops:
  0.6 27.9 %shard_map.130 = (f32[1,3,8,256]{3,2,1,0:T(8,128)}, f32[32,256]{1,0:T(8,128)}, s32[2,512]{1,0:T(2,128)}, f32[2,16,128]{2,1,0:T(8,128)}) custom-call(f32[3,2048]{1,0:T(4,128)} %means.1, f32[3,2048]{1,0:T(4,128)} %log_scales.1, f32[1,2048]{1,0:T(1,128)} %quat_w.1, f32[3,2048]{1,0:T(4,128)} %quat_v.1, f32[1,2048]{1,0:T(1,128)} %opacity.1, f32[48,2048]{1,0:T(8,128)} %sh_hbm.1, ...), custom_call_target="tpu_custom_call" | custom-call | tf_op jit(solution)/shard_map/pallas_call | solution.py:853
  28.6 2.3 %shard_map.131 = (f32[1,3,8,256]{3,2,1,0:T(8,128)}, f32[59,2048]{1,0:T(8,128)}, f32[2,10]{1,0:T(2,128)}) custom-call(f32[3,2048]{1,0:T(4,128)} %means.1, f32[3,2048]{1,0:T(4,128)} %log_scales.1, f32[1,2048]{1,0:T(1,128)} %quat_w.1, f32[3,2048]{1,0:T(4,128)} %quat_v.1, f32[1,2048]{1,0:T(1,128)} %opacity.1, f32[2,10]{1,0:T(2,128)} %cams.3, ...), custom_call_target="tpu_custom_call" | custom-call | tf_op jit(solution)/shard_map/pallas_call | solution.py:907
